TPU v7x, 32 devices: a whole 2x2x4 slice. The times are simulated.
32 devices in a mesh: samp: 8 (over y, x, core), var: 4 (over z).
Axes of the slice: x: 2, y: 2, z: 4, core: 2. Of those that a mesh axis runs over, the one named last changes fastest.
Arguments:
- genotypes: bfloat16 [8192, 16384], P('samp', 'var'), may hold values from 0 to 2, as said below
- col_mean: float32 [16384], P('var'), may hold values from 0.1 to 1, as said below
- inv_scale: float32 [16384], P('var'), may hold values from 1.4 to 3.25, as said below
- targets: float32 [8192], P('samp'), may hold values from -6 to 6
- probes: float32 [8192, 7], P('samp'), may hold values from -6 to 6
- delta: float32 [1], replicated, may hold values from 0.5 to 2
Outputs:
- solution: float32 [8192, 8], P('samp')
- assoc: float32 [16384], P('var')
Inputs may be any that keep to these rules, and one draw needn't show every extreme that they name: `genotypes`: dosages 0, 1 or 2, drawn per variant from an allele frequency f of 0.05 to 0.5. `col_mean`: 2 f for the variant's allele frequency f. `inv_scale`: 1 / sqrt(2 f (1 - f)) for the same frequency f.
All inputs are finite; a program needn't handle non-finite values.
Results may differ from a plain program's by a relative error of at most 0.0003.
Values sent between devices are 32-bit elements; how exact they have to be, the bound alone decides.
No kernel may reach another device: no remote copies, remote signals or barrier semaphores. Data moves between devices by JAX's collectives and lax.ppermute only.
A program may use at most 64 MiB of HBM per device.

v0:
```python
import jax
import jax.numpy as jnp
from jax import lax
from jax.sharding import PartitionSpec as P

ITERS = 2


HI = lax.Precision.HIGHEST


def column_norms(vectors):
    return lax.psum(jnp.sum(vectors * vectors, 0), "samp")


def per_device(genotypes, col_mean, inv_scale, targets, probes, delta):
    n_total = genotypes.shape[0] * lax.axis_size("samp")
    m_total = genotypes.shape[1] * lax.axis_size("var")
    shift = delta[0]
    dense = genotypes.astype(jnp.float32)
    rhs = jnp.concatenate([targets[:, None], probes], 1)

    def transposed(vectors):
        return lax.dot_general(
            dense,
            vectors,
            (((0,), (0,)), ((), ())),
            precision=HI,
            preferred_element_type=jnp.float32,
        )

    solution = jnp.zeros_like(rhs)
    residual = rhs
    direction = rhs
    nothing = jnp.zeros_like(rhs)
    norm_now = column_norms(residual)
    for step in range(ITERS):
        across_part = transposed(direction)
        totals = jnp.sum(direction, 0)
        across_squares = jnp.sum(direction * direction, 0)
        inner = jnp.sum(direction * nothing, 0)
        across_part, totals, across_squares, inner = lax.psum(
            (across_part, totals, across_squares, inner), "samp"
        )
        columns, squares, inner = (
            inv_scale[:, None] * (across_part - col_mean[:, None] * totals[None, :]),
            across_squares,
            inner,
        )
        scaled = inv_scale[:, None] * columns
        offset = jnp.dot(col_mean, scaled, precision=HI, preferred_element_type=jnp.float32)
        partial_value = (
            jnp.dot(dense, scaled, precision=HI, preferred_element_type=jnp.float32)
            - offset[None, :]
        )
        summed, column_squares = lax.psum((partial_value, jnp.sum(columns * columns, 0)), "var")
        image = summed / m_total + shift * direction
        curving = column_squares / m_total + shift * squares
        image, curving = (image, curving)
        alpha = norm_now / curving
        solution = solution + alpha[None, :] * direction
        if step + 1 < ITERS:
            residual = residual - alpha[None, :] * image
            norm_next = column_norms(residual)
            direction = residual + (norm_next / norm_now)[None, :] * direction
            norm_now = norm_next
    target_sol = solution[:, 0:1]
    part = transposed(target_sol)[:, 0]
    part, total = lax.psum((part, jnp.sum(target_sol)), "samp")
    first = inv_scale * (part - col_mean * total)
    assoc = first / jnp.sqrt(jnp.float32(n_total))
    return (solution, assoc)


def solution(mesh):
    placed = (P("samp", "var"), P("var"), P("var"), P("samp"), P("samp", None), P())
    return jax.shard_map(
        per_device,
        mesh=mesh,
        in_specs=placed,
        out_specs=(P("samp", None), P("var")),
        check_vma=False,
    )
```

profile of v0, /device:TPU:0, one launch (start us, length us, event | category | flops | bytes accessed | tf_op | source)
XLA Modules:
  0.0 220.3 jit_solution(17025808727799073871)
XLA Ops:
  7.2 0.0 copy-start
  7.2 0.0 copy-start.4
  7.2 0.0 copy-start.2
  7.2 0.0 copy-start.3
  7.2 0.0 all-reduce.7.cloned.1.call-start
  7.3 7.4 %convolution_bitcast_fusion.1 = f32[4096,8]{0,1:T(8,128)} fusion(bf16[1024,4096]{1,0:T(8,128)(2,1)} %param.6, f32[1024,7]{0,1:T(8,128)} %param.10, f32[1024,1]{0,1:T(1,128)} %bitcast.24), kind=kOutput, calls=%fused_computation.1 | convolution fusion | flops 402661376 | bytes 8552448 | tf_op jit(solution)/shard_map/dot_general | solution.py:24
  14.7 0.0 all-reduce.7.cloned.1.call-update
  14.7 0.0 all-reduce.9.cloned.1.call-start
  14.8 0.0 copy-done
  14.8 0.0 copy-done.4
  14.8 0.2 multiply_reduce_fusion.4
  14.9 15.1 %all-reduce.2 = (f32[8]{0:T(128)S(1)}, f32[8]{0:T(128)S(1)}) all-reduce(f32[8]{0:T(128)S(1)} %get-tuple-element.3, f32[8]{0:T(128)S(1)} %get-tuple-element.2), channel_id=1, replica_groups=mesh['samp'=8,'var'=4] {'samp'}, use_global_device_ids=true, to_apply=%region_4.0 | all-reduce | flops 16 | bytes 128 | tf_op jit(solution)/shard_map/psum | solution.py:42
  30.7 39.8 %all-reduce.7.cloned.1.call-done = f32[4096,8]{0,1:T(8,128)} async-done(((f32[4096,8]{0,1:T(8,128)}), f32[4096,8]{0,1:T(8,128)}) %all-reduce.7.cloned.1.call-update) | async-done | bytes 131088 | tf_op jit(solution)/shard_map/psum | solution.py:42
  70.5 0.0 copy-done.2
  70.5 0.0 copy-done.3
  70.5 1.1 multiply_reduce_fusion.1
  71.6 1.3 convolution_bitcast_fusion.2
  72.9 8.9 %fusion = f32[1024,8]{0,1:T(8,128)S(1)} fusion(bf16[1024,4096]{1,0:T(8,128)(2,1)} %param.6, f32[4096,8]{0,1:T(8,128)} %all-reduce.7.cloned.1.call-done, f32[8]{0:T(128)S(1)} %get-tuple-element.10, f32[4096]{0:T(1024)S(1)} %copy-done.2, f32[4096]{0:T(1024)S(1)} %copy-done.3, f32[8]{0:T(128)S(1)} %convolution_bitcast_fusion.2), kind=kOutput, calls=%fused_computation.3 | convolution fusion | flops 402792448 | bytes 8585280 | tf_op jit(solution)/shard_map/dot_general | solution.py:53
  81.9 19.3 %all-reduce.3 = (f32[1024,8]{0,1:T(8,128)S(1)}, f32[8]{0:T(128)S(1)}) all-reduce(f32[1024,8]{0,1:T(8,128)S(1)} %fusion, f32[8]{0:T(128)S(1)} %multiply_reduce_fusion.1), channel_id=1, replica_groups=mesh['samp'=8,'var'=4] {'var'}, use_global_device_ids=true, to_apply=%region_7.0 | all-reduce | flops 8200 | bytes 65600 | tf_op jit(solution)/shard_map/psum | solution.py:56
  101.2 0.2 multiply_reduce_fusion.3
  101.4 11.8 %psum.92 = f32[8]{0:T(128)S(1)} all-reduce(f32[8]{0:T(128)S(1)} %multiply_reduce_fusion.3), channel_id=1, replica_groups=mesh['samp'=8,'var'=4] {'samp'}, use_global_device_ids=true, to_apply=%region_9.0 | all-reduce | flops 8 | bytes 64 | tf_op jit(solution)/shard_map/psum | solution.py:13
  113.2 0.2 fusion.12
  113.5 6.3 %convolution_bitcast_fusion = f32[4096,8]{0,1:T(8,128)} fusion(f32[1024,8]{0,1:T(8,128)S(1)} %get-tuple-element.14, bf16[1024,4096]{1,0:T(8,128)(2,1)} %param.6), kind=kOutput, calls=%fused_computation | convolution fusion | flops 402653184 | bytes 8552448 | tf_op jit(solution)/shard_map/dot_general | solution.py:24
  119.8 0.0 all-reduce.9.cloned.1.call-update
  119.8 11.8 %all-reduce.1 = (f32[8]{0:T(128)S(1)}, f32[8]{0:T(128)S(1)}) all-reduce(f32[8]{0:T(128)S(1)} %get-tuple-element.5, f32[8]{0:T(128)S(1)} %get-tuple-element.4), channel_id=1, replica_groups=mesh['samp'=8,'var'=4] {'samp'}, use_global_device_ids=true, to_apply=%region_16.0 | all-reduce | flops 16 | bytes 128 | tf_op jit(solution)/shard_map/psum | solution.py:42
  131.6 37.9 %all-reduce.9.cloned.1.call-done = f32[4096,8]{0,1:T(8,128)} async-done(((f32[4096,8]{0,1:T(8,128)}), f32[4096,8]{0,1:T(8,128)}) %all-reduce.9.cloned.1.call-update) | async-done | bytes 131088 | tf_op jit(solution)/shard_map/psum | solution.py:42
  169.5 1.1 multiply_reduce_fusion
  170.7 11.7 %psum.95 = f32[8]{0:T(128)S(1)} all-reduce(f32[8]{0:T(128)S(1)} %multiply_reduce_fusion), channel_id=1, replica_groups=mesh['samp'=8,'var'=4] {'var'}, use_global_device_ids=true, to_apply=%region_14.0 | all-reduce | flops 8 | bytes 64 | tf_op jit(solution)/shard_map/psum | solution.py:56
  182.4 0.1 multiply_add_fusion
  182.4 0.0 copy-start.1
  182.4 0.6 slice_reduce_fusion
  183.0 5.7 %fusion.9 = f32[1,4096]{1,0:T(1,128)S(1)} fusion(bf16[1024,4096]{1,0:T(8,128)(2,1)} %param.6, f32[1024,8]{0,1:T(8,128)S(1)} %multiply_add_fusion), kind=kOutput, calls=%fused_computation.25 | convolution fusion | flops 50331648 | bytes 8409088 | tf_op jit(solution)/shard_map/dot_general | solution.py:24
  188.7 23.5 %all-reduce = (f32[4096]{0:T(1024)S(1)}, f32[]{:T(128)}) all-reduce(f32[4096]{0:T(1024)S(1)} %bitcast.29, f32[]{:T(128)} %slice_reduce_fusion), channel_id=1, replica_groups=mesh['samp'=8,'var'=4] {'samp'}, use_global_device_ids=true, to_apply=%region_17.0 | all-reduce | flops 4097 | bytes 32776 | tf_op jit(solution)/shard_map/psum | solution.py:69
  212.2 1.3 multiply_multiply_fusion
  213.5 0.0 copy-done.1
  (3 shorter events, 0.0 us)
Async XLA Ops:
  7.2 7.6 %copy-start = (f32[1024,7]{0,1:T(8,128)S(1)}, f32[1024,7]{0,1:T(8,128)}, u32[]{:S(2)}) copy-start(f32[1024,7]{0,1:T(8,128)} %param.10) | copy-start | bytes 86020
  7.2 7.6 %copy-start.4 = (f32[1024]{0:T(1024)S(1)}, f32[1024]{0:T(1024)}, u32[]{:S(2)}) copy-start(f32[1024]{0:T(1024)} %param.9) | copy-start | bytes 12292
  7.2 63.3 %copy-start.2 = (f32[4096]{0:T(1024)S(1)}, f32[4096]{0:T(1024)}, u32[]{:S(2)}) copy-start(f32[4096]{0:T(1024)} %param.7) | copy-start | bytes 49156
  7.2 63.3 %copy-start.3 = (f32[4096]{0:T(1024)S(1)}, f32[4096]{0:T(1024)}, u32[]{:S(2)}) copy-start(f32[4096]{0:T(1024)} %param.8) | copy-start | bytes 49156
  7.2 63.3 %all-reduce.7.cloned.1.call-start = ((), (), s32[]{:S(2)}) async-start(), calls=%async_computation | async-start | bytes 262144 | tf_op jit(solution)/shard_map/psum | solution.py:42
  14.7 154.8 %all-reduce.9.cloned.1.call-start = ((), (), s32[]{:S(2)}) async-start(), calls=%async_computation.1 | async-start | bytes 262144 | tf_op jit(solution)/shard_map/psum | solution.py:42
  182.4 31.0 %copy-start.1 = (f32[1024,8]{0,1:T(8,128)}, f32[1024,8]{0,1:T(8,128)S(1)}, u32[]{:S(2)}) copy-start(f32[1024,8]{0,1:T(8,128)S(1)} %multiply_add_fusion) | copy-start | bytes 98308
Sparse Core Ops, SparseCore 0:
  14.8 55.6 all-reduce.6
  119.9 49.5 all-reduce.8
where the time goes:
time: 221 us; the launch traced here: 220 us
  blocking collectives  93.2 us (42%)
  waiting for transfers between devices  77.7 us (35%)
  matrix products  29.7 us (13%)
  between operations  14.8 us (7%)
  other arithmetic  4.83 us (2%)
    psum x2, waiting for transfers between devices, per_device(): lax.psum((across_part, totals, across_squares, inner), 'samp')  77.7 us
    psum x2, blocking collectives, per_device(): lax.psum((partial_value, jnp.sum(columns * columns, 0)), 'var')  31 us
    psum x2, blocking collectives, per_device(): lax.psum((across_part, totals, across_squares, inner), 'samp')  27 us
    psum x1, blocking collectives, per_device(): part, total = lax.psum((part, jnp.sum(target_sol)), 'samp')  23.5 us
    dot_general x3, matrix products, transposed(): lax.dot_general(dense, vectors, (((0,), (0,)), ((), ())), precision=HI, p...  19.4 us
    psum x1, blocking collectives, column_norms(): return lax.psum(jnp.sum(vectors * vectors, 0), 'samp')  11.8 us
    dot_general x1, matrix products, per_device(): jnp.dot(dense, scaled, precision=HI, preferred_element_type=jnp.float32)  8.94 us
  transfers between devices with their start and end apart: 2, of which 2 were waited for; matrix products, arithmetic and copies ran while one was open for 0% of the time, Pallas kernels for 0%

commit v1 on v0

v1 whole, which is shorter than its diff:
```python
import functools

import jax
import jax.numpy as jnp
from jax import lax
from jax.experimental import pallas as pl
from jax.experimental.pallas import tpu as pltpu
from jax.sharding import PartitionSpec as P

LANES = 128
ROW_CHUNKS = 8
LIMIT = 40 << 20
F32 = jnp.float32
BF16 = jnp.bfloat16


def in_two(values):
    high = values.astype(BF16).astype(F32)
    return jnp.concatenate([high, values - high], 0).astype(BF16)


def summed(product):
    rows = product.shape[0] // 2
    return product[:rows] + product[rows:]


def tail_of(*columns):
    rows = columns[0].shape[0]
    lane = lax.broadcasted_iota(jnp.int32, (rows, LANES), 1)
    tail = jnp.zeros((rows, LANES), F32)
    for at, column in enumerate(columns):
        tail = jnp.where(lane == at, column, tail)
    return tail


def row_sum(values):
    return jnp.sum(values, 1, keepdims=True)


def put_halves(core, product, tail, own, other):
    half = product.shape[1] // 2

    def put(low, high):
        low[:, :half] = product[:, :half]
        high[:, :half] = product[:, half:]

    @pl.when(core == 0)
    def _():
        put(own, other)

    @pl.when(core == 1)
    def _():
        put(other, own)

    own[:, half:] = tail
    other[:, half:] = tail


def first_kernel(targets, probes, genotypes, held, rhs_out, own, other, sems):
    rows = genotypes.shape[0] // ROW_CHUNKS
    copies = [
        pltpu.make_async_copy(
            genotypes.at[pl.ds(at * rows, rows)], held.at[pl.ds(at * rows, rows)], sems.at[at]
        )
        for at in range(ROW_CHUNKS)
    ]
    for copy in copies:
        copy.start()
    rhs = jnp.concatenate([targets[...], probes[...]], 0)
    rhs_out[...] = rhs
    pieces = in_two(rhs)
    total = None
    for at, copy in enumerate(copies):
        copy.wait()
        part = jnp.dot(
            pieces[:, at * rows : (at + 1) * rows],
            held[pl.ds(at * rows, rows), :],
            preferred_element_type=F32,
        )
        total = part if total is None else total + part
    tail = tail_of(row_sum(rhs), row_sum(rhs * rhs))
    put_halves(lax.axis_index("samp") % 2, summed(total), tail, own, other)


def joined(own, mate):
    half = own.shape[1] - LANES
    core = lax.axis_index("samp") % 2
    mine, theirs = own[:, :half], mate[:, :half]
    low = jnp.where(core == 0, mine, theirs)
    high = jnp.where(core == 0, theirs, mine)
    return jnp.concatenate([low, high], 1)


def along_kernel(own, mate, col_mean, inv_scale, held, columns_out, part_out):
    half = own.shape[1] - LANES
    samples = held.shape[0]
    totals = own[:, half : half + 1]
    columns = inv_scale[...] * (joined(own, mate) - col_mean[...] * totals)
    columns_out[...] = columns
    scaled = inv_scale[...] * columns
    offset = row_sum(col_mean[...] * scaled)
    product = summed(
        lax.dot_general(
            in_two(scaled), held[...], (((1,), (1,)), ((), ())), preferred_element_type=F32
        )
    )
    part_out[:, :samples] = product - offset
    part_out[:, samples:] = tail_of(row_sum(columns * columns))


def second_kernel(m_total, delta, rhs, first, held, *rest):
    *parts, residual_out, alpha_out, own, other = rest
    samples = held.shape[0]
    image = functools.reduce(jnp.add, [part[...] for part in parts])
    half = first.shape[1] - LANES
    squares = first[:, half + 1 : half + 2]
    shift = delta[0]
    curving = image[:, samples : samples + 1] / m_total + shift * squares
    alpha = squares / curving
    direction = rhs[...]
    residual = direction - alpha * (image[:, :samples] / m_total + shift * direction)
    residual_out[...] = residual
    alpha_out[...] = jnp.broadcast_to(alpha, alpha_out.shape)
    product = summed(jnp.dot(in_two(residual), held[...], preferred_element_type=F32))
    tail = tail_of(
        row_sum(residual), row_sum(residual * residual), row_sum(residual * direction)
    )
    put_halves(lax.axis_index("samp") % 2, product, tail, own, other)


def third_kernel(own, mate, first, columns, col_mean, inv_scale, columns_out, part_out):
    half = own.shape[1] - LANES
    ratio = own[:, half + 1 : half + 2] / first[:, half + 1 : half + 2]
    fresh = inv_scale[...] * (joined(own, mate) - col_mean[...] * own[:, half : half + 1])
    fresh = fresh + ratio * columns[...]
    columns_out[...] = fresh[:1]
    part_out[...] = tail_of(row_sum(fresh * fresh))


def last_kernel(
    m_total, n_total, delta, rhs, residual, alpha, first, second, columns, fresh, *rest
):
    *parts, solution_out, assoc_out = rest
    half = first.shape[1] - LANES
    shift = delta[0]
    norm_first = first[:, half + 1 : half + 2]
    norm_now = second[:, half + 1 : half + 2]
    across = second[:, half + 2 : half + 3]
    ratio = norm_now / norm_first
    squares = norm_now + ratio * (2.0 * across + ratio * norm_first)
    column_squares = functools.reduce(jnp.add, [part[...] for part in parts])[:, :1]
    beta = norm_now / (column_squares / m_total + shift * squares)
    alpha = alpha[:, :1]
    direction = residual[...] + ratio * rhs[...]
    solution_out[...] = alpha * rhs[...] + beta * direction
    assoc_out[...] = (alpha[:1] * columns[:1, :] + beta[:1] * fresh[...]) / jnp.sqrt(
        jnp.float32(n_total)
    )


def per_device(genotypes, col_mean, inv_scale, targets, probes, delta):
    samples, variants = genotypes.shape
    samp, var = lax.axis_size("samp"), lax.axis_size("var")
    n_total, m_total = samples * samp, variants * var
    cols = probes.shape[1] + 1
    half = variants // 2

    vmem = pl.BlockSpec(memory_space=pltpu.VMEM)
    smem = pl.BlockSpec(memory_space=pltpu.SMEM)
    hbm = pl.BlockSpec(memory_space=pl.ANY)
    params = pltpu.CompilerParams(vmem_limit_bytes=LIMIT)

    def array(*shape):
        return jax.ShapeDtypeStruct(shape, F32)

    def swapped(values, axis, flip):
        size = lax.axis_size(axis)
        return lax.ppermute(values, axis, [(at, at ^ flip) for at in range(size)])

    def gathered(values, axis, first_bit):
        bit, size = first_bit, lax.axis_size(axis)
        while True:
            flips = [bit, 2 * bit, 3 * bit] if 2 * bit < size else [bit] * (bit < size)
            terms = [values] + [swapped(values, axis, flip) for flip in flips]
            bit *= 4
            if bit >= size:
                return terms
            values = functools.reduce(jnp.add, terms)

    def summed_over_samp(own, other):
        own = own + swapped(other, "samp", 1)
        return functools.reduce(jnp.add, gathered(own, "samp", 2))

    col_mean, inv_scale = col_mean[None, :], inv_scale[None, :]
    held, rhs, own, other = pl.pallas_call(
        first_kernel,
        in_specs=[vmem, vmem, hbm],
        out_specs=[vmem] * 4,
        out_shape=[
            pltpu.VMEM((samples, variants), BF16),
            array(cols, samples),
            array(cols, half + LANES),
            array(cols, half + LANES),
        ],
        scratch_shapes=[pltpu.SemaphoreType.DMA((ROW_CHUNKS,))],
        compiler_params=params,
        name="across_first",
    )(targets[None, :], probes.T, genotypes)
    held = pltpu.with_memory_space_constraint(held, pltpu.VMEM)
    first = summed_over_samp(own, other)
    mate = swapped(first, "samp", 1)
    columns, part = pl.pallas_call(
        along_kernel,
        in_specs=[vmem] * 5,
        out_specs=[vmem] * 2,
        out_shape=[array(cols, variants), array(cols, samples + LANES)],
        compiler_params=params,
        name="along",
    )(first, mate, col_mean, inv_scale, held)
    parts = gathered(part, "var", 1)
    residual, alpha, own, other = pl.pallas_call(
        functools.partial(second_kernel, m_total),
        in_specs=[smem] + [vmem] * (3 + len(parts)),
        out_specs=[vmem] * 4,
        out_shape=[
            array(cols, samples),
            array(cols, LANES),
            array(cols, half + LANES),
            array(cols, half + LANES),
        ],
        compiler_params=params,
        name="across_second",
    )(delta, rhs, first, held, *parts)
    second = summed_over_samp(own, other)
    mate = swapped(second, "samp", 1)
    fresh, part = pl.pallas_call(
        third_kernel,
        in_specs=[vmem] * 6,
        out_specs=[vmem] * 2,
        out_shape=[array(1, variants), array(cols, LANES)],
        compiler_params=params,
        name="columns",
    )(second, mate, first, columns, col_mean, inv_scale)
    parts = gathered(part, "var", 1)
    solved, assoc = pl.pallas_call(
        functools.partial(last_kernel, m_total, n_total),
        in_specs=[smem] + [vmem] * (7 + len(parts)),
        out_specs=[vmem] * 2,
        out_shape=[array(cols, samples), array(1, variants)],
        compiler_params=params,
        name="combine",
    )(delta, rhs, residual, alpha, first, second, columns, fresh, *parts)
    return (solved.T, assoc[0])


def solution(mesh):
    placed = (P("samp", "var"), P("var"), P("var"), P("samp"), P("samp", None), P())
    return jax.shard_map(
        per_device,
        mesh=mesh,
        in_specs=placed,
        out_specs=(P("samp", None), P("var")),
        check_vma=False,
    )
```

time: 221 us -> 46.5 us (0.21)
  blocking collectives: 93.2 us -> 0 us
  waiting for transfers between devices: 77.7 us -> 17.3 us
  matrix products: 29.7 us -> 0 us
  starting transfers between devices: 0.08 us -> 17.5 us
  between operations: 14.8 us -> 1.36 us
  Pallas kernels: 0 us -> 8.6 us
  other arithmetic: 4.83 us -> 0.07 us
    psum x6 -> x0, blocking collectives: 93.2 us -> none  [the longest x2 31 us: per_device(): lax.psum((partial_value, jnp.sum(columns * columns, 0)), 'var')]
    psum x2 -> x0, waiting for transfers between devices: 77.7 us -> none  [per_device(): lax.psum((across_part, totals, across_squares, inner), 'samp')]
    dot_general x5 -> x0, matrix products: 29.7 us -> none  [the longest x3 19.4 us: transposed(): lax.dot_general(dense, vectors, (((0,), (0,)), ((), ())), precision=HI, p...]
    ppermute x0 -> x16, starting transfers between devices: none -> 17.5 us  [swapped(): return lax.ppermute(values, axis, [(at, at ^ flip) for at in range(size)])]
    ppermute x0 -> x16, waiting for transfers between devices: none -> 17.3 us  [swapped(): return lax.ppermute(values, axis, [(at, at ^ flip) for at in range(size)])]
    pallas_call x0 -> x5, Pallas kernels: none -> 8.6 us  [the longest x1 3.73 us: per_device(): pl.pallas_call(first_kernel, in_specs=[vmem, vmem, hbm], out_specs=[vmem]...]
    reduce_sum x6 -> x0, other arithmetic: 3.43 us -> none  [the longest x2 2.24 us: per_device(): jnp.sum(columns * columns, 0)]
  transfers between devices with their start and end apart: 2 -> 16, of which waited for: 2 -> 14; matrix products, arithmetic and copies ran while one was open for 0% -> 0% of each run, Pallas kernels for 0% -> 0%
where the time goes in v1:
time: 46.5 us; the launch traced here: 46.3 us
  starting transfers between devices  17.5 us (38%)
  waiting for transfers between devices  17.3 us (37%)
  Pallas kernels  8.6 us (18%)
  local copies, waits for them, and re-layouts  1.46 us (3%)
  between operations  1.36 us (3%)
    ppermute x16, starting transfers between devices, swapped(): return lax.ppermute(values, axis, [(at, at ^ flip) for at in range(size)])  17.5 us
    ppermute x16, waiting for transfers between devices, swapped(): return lax.ppermute(values, axis, [(at, at ^ flip) for at in range(size)])  17.3 us
    pallas_call x1, Pallas kernels, per_device(): pl.pallas_call(first_kernel, in_specs=[vmem, vmem, hbm], out_specs=[vmem]...  3.73 us
    pallas_call x1, Pallas kernels, per_device(): pl.pallas_call(along_kernel, in_specs=[vmem] * 5, out_specs=[vmem] * 2, o...  2.28 us
    unnamed x8, local copies, waits for them, and re-layouts  1.46 us
    pallas_call x1, Pallas kernels, per_device(): pl.pallas_call(functools.partial(second_kernel, m_total), in_specs=[smem]...  1.39 us
    pallas_call x1, Pallas kernels, per_device(): pl.pallas_call(functools.partial(last_kernel, m_total, n_total), in_specs...  0.99 us
  transfers between devices with their start and end apart: 16, of which 14 were waited for; matrix products, arithmetic and copies ran while one was open for 0% of the time, Pallas kernels for 0%

profile of v1, /device:TPU:0, one launch (start us, length us, event | category | flops | bytes accessed | tf_op | source)
XLA Modules:
  0.0 46.3 jit_solution(3742261211323891169)
XLA Ops:
  0.6 0.0 copy-start.1
  0.6 0.0 copy-start
  0.7 0.0 copy-start.2
  0.7 0.8 %copy-done.2 = f32[1024,7]{0,1:T(8,128)S(1)} copy-done((f32[1024,7]{0,1:T(8,128)S(1)}, f32[1024,7]{0,1:T(8,128)}, u32[]{:S(2)}) %copy-start.2) | copy-done | bytes 28696
  1.4 0.0 copy-start.3
  1.4 0.7 %copy-done.3 = f32[1024]{0:T(1024)S(1)} copy-done((f32[1024]{0:T(1024)S(1)}, f32[1024]{0:T(1024)}, u32[]{:S(2)}) %copy-start.3) | copy-done | bytes 4120
  2.1 3.7 %across_first.1 = (bf16[1024,4096]{1,0:T(8,128)(2,1)S(1)}, f32[8,1024]{1,0:T(8,128)S(1)}, f32[8,2176]{1,0:T(8,128)S(1)}, f32[8,2176]{1,0:T(8,128)S(1)}) custom-call(f32[1,1024]{1,0:T(1,128)S(1)} %bitcast.11, f32[7,1024]{1,0:T(8,128)S(1)} %bitcast.10, bf16[1024,4096]{1,0:T(8,128)(2,1)} %genotypes.1), custom_call_target="tpu_custom_call" | custom-call | tf_op jit(solution)/shard_map/across_first/pallas_call | solution.py:195
  5.8 0.5 %collective-permute-start = (f32[8,2176]{1,0:T(8,128)S(1)}, f32[8,2176]{1,0:T(8,128)S(1)}, u32[]{:S(2)}, u32[]{:S(2)}) collective-permute-start(f32[8,2176]{1,0:T(8,128)S(1)} %get-tuple-element.18), channel_id=1, source_target_pairs={{0,4},{4,0},{8,12},{12,8},{16,20},{20,16},{24,28},{28,24},{1,5},{5... | collective-permute-start | bytes 208904 | tf_op jit(solution)/shard_map/ppermute | solution.py:178
  6.4 0.9 %collective-permute-done = f32[8,2176]{1,0:T(8,128)S(1)} collective-permute-done((f32[8,2176]{1,0:T(8,128)S(1)}, f32[8,2176]{1,0:T(8,128)S(1)}, u32[]{:S(2)}, u32[]{:S(2)}) %collective-permute-start) | collective-permute-done | bytes 69664 | tf_op jit(solution)/shard_map/ppermute | solution.py:178
  7.3 3.9 %collective-permute-start.3 = (f32[8,2176]{1,0:T(8,128)S(1)}, f32[8,2176]{1,0:T(8,128)S(1)}, u32[]{:S(2)}, u32[]{:S(2)}) collective-permute-start(f32[8,2176]{1,0:T(8,128)S(1)} %add.24), channel_id=1, source_target_pairs={{0,24},{4,28},{8,16},{12,20},{16,8},{20,12},{24,0},{28,4},{1,25},{... | collective-permute-start | bytes 208904 | tf_op jit(solution)/shard_map/ppermute | solution.py:178
  11.1 0.5 %collective-permute-start.2 = (f32[8,2176]{1,0:T(8,128)S(1)}, f32[8,2176]{1,0:T(8,128)S(1)}, u32[]{:S(2)}, u32[]{:S(2)}) collective-permute-start(f32[8,2176]{1,0:T(8,128)S(1)} %add.24), channel_id=1, source_target_pairs={{0,16},{4,20},{8,24},{12,28},{16,0},{20,4},{24,8},{28,12},{1,17},{... | collective-permute-start | bytes 208904 | tf_op jit(solution)/shard_map/ppermute | solution.py:178
  11.7 0.1 collective-permute-start.1
  11.8 1.9 %collective-permute-done.3 = f32[8,2176]{1,0:T(8,128)S(1)} collective-permute-done((f32[8,2176]{1,0:T(8,128)S(1)}, f32[8,2176]{1,0:T(8,128)S(1)}, u32[]{:S(2)}, u32[]{:S(2)}) %collective-permute-start.3) | collective-permute-done | bytes 69664 | tf_op jit(solution)/shard_map/ppermute | solution.py:178
  13.7 1.8 %collective-permute-done.2 = f32[8,2176]{1,0:T(8,128)S(1)} collective-permute-done((f32[8,2176]{1,0:T(8,128)S(1)}, f32[8,2176]{1,0:T(8,128)S(1)}, u32[]{:S(2)}, u32[]{:S(2)}) %collective-permute-start.2) | collective-permute-done | bytes 69664 | tf_op jit(solution)/shard_map/ppermute | solution.py:178
  15.5 0.5 %collective-permute-done.1 = f32[8,2176]{1,0:T(8,128)S(1)} collective-permute-done((f32[8,2176]{1,0:T(8,128)S(1)}, f32[8,2176]{1,0:T(8,128)S(1)}, u32[]{:S(2)}, u32[]{:S(2)}) %collective-permute-start.1) | collective-permute-done | bytes 69664 | tf_op jit(solution)/shard_map/ppermute | solution.py:178
  16.0 0.1 collective-permute-start.4
  16.1 1.2 %collective-permute-done.4.mate = f32[8,2176]{1,0:T(8,128)S(1)} collective-permute-done((f32[8,2176]{1,0:T(8,128)S(1)}, f32[8,2176]{1,0:T(8,128)S(1)}, u32[]{:S(2)}, u32[]{:S(2)}) %collective-permute-start.4) | collective-permute-done | bytes 69664 | tf_op jit(solution)/shard_map/ppermute | solution.py:178
  17.3 0.0 copy-done.1
  17.3 0.0 copy-done
  17.3 2.3 %along.1 = (f32[8,4096]{1,0:T(8,128)S(1)}, f32[8,1152]{1,0:T(8,128)S(1)}) custom-call(f32[8,2176]{1,0:T(8,128)S(1)} %add_add_fusion.1.own.first, f32[8,2176]{1,0:T(8,128)S(1)} %collective-permute-done.4.mate, f32[1,4096]{1,0:T(1,128)S(1)} %bitcast.6, f32[1,4096]{1,0:T(1,128)S(1)} %bitcast.8, bf16[1024,4096]{1,0:T(8,128)(2,1)S(1)} %get-tuple-element.19.held), custom_call_target="tpu_custom_call" | custom-call | tf_op jit(solution)/shard_map/along/pallas_call | solution.py:212
  19.6 3.6 %collective-permute-start.7 = (f32[8,1152]{1,0:T(8,128)S(1)}, f32[8,1152]{1,0:T(8,128)S(1)}, u32[]{:S(2)}, u32[]{:S(2)}) collective-permute-start(f32[8,1152]{1,0:T(8,128)S(1)} %get-tuple-element.20.rest_0_), channel_id=1, source_target_pairs={{0,3},{1,2},{2,1},{3,0},{4,7},{5,6},{6,5},{7,4},{8,11},{9,10},{10,... | collective-permute-start | bytes 110600 | tf_op jit(solution)/shard_map/ppermute | solution.py:178
  23.2 0.0 collective-permute-start.6
  23.2 0.8 %collective-permute-start.5 = (f32[8,1152]{1,0:T(8,128)S(1)}, f32[8,1152]{1,0:T(8,128)S(1)}, u32[]{:S(2)}, u32[]{:S(2)}) collective-permute-start(f32[8,1152]{1,0:T(8,128)S(1)} %get-tuple-element.20.rest_0_), channel_id=1, source_target_pairs={{0,1},{1,0},{2,3},{3,2},{4,5},{5,4},{6,7},{7,6},{8,9},{9,8},{10,11... | collective-permute-start | bytes 110600 | tf_op jit(solution)/shard_map/ppermute | solution.py:178
  24.7 0.7 %collective-permute-done.7.rest_3_ = f32[8,1152]{1,0:T(8,128)S(1)} collective-permute-done((f32[8,1152]{1,0:T(8,128)S(1)}, f32[8,1152]{1,0:T(8,128)S(1)}, u32[]{:S(2)}, u32[]{:S(2)}) %collective-permute-start.7) | collective-permute-done | bytes 36896 | tf_op jit(solution)/shard_map/ppermute | solution.py:178
  25.4 2.7 %collective-permute-done.6.rest_2_ = f32[8,1152]{1,0:T(8,128)S(1)} collective-permute-done((f32[8,1152]{1,0:T(8,128)S(1)}, f32[8,1152]{1,0:T(8,128)S(1)}, u32[]{:S(2)}, u32[]{:S(2)}) %collective-permute-start.6) | collective-permute-done | bytes 36896 | tf_op jit(solution)/shard_map/ppermute | solution.py:178
  28.1 0.0 collective-permute-done.5.rest_1_
  28.1 1.4 %across_second.1 = (f32[8,1024]{1,0:T(8,128)S(1)}, f32[8,128]{1,0:T(8,128)S(1)}, f32[8,2176]{1,0:T(8,128)S(1)}, f32[8,2176]{1,0:T(8,128)S(1)}) custom-call(f32[1]{0:T(128)S(6)} %copy.8.delta, f32[8,1024]{1,0:T(8,128)S(1)} %get-tuple-element.16.rhs, f32[8,2176]{1,0:T(8,128)S(1)} %add_add_fusion.1.own.first, bf16[1024,4096]{1,0:T(8,128)(2,1)S(1)} %get-tuple-element.19.held, ...), custom_call_target="tpu_custom_call" | custom-call | tf_op jit(solution)/shard_map/across_second/pallas_call | solution.py:221
  29.5 0.0 collective-permute-start.8
  29.5 1.3 %collective-permute-done.8 = f32[8,2176]{1,0:T(8,128)S(1)} collective-permute-done((f32[8,2176]{1,0:T(8,128)S(1)}, f32[8,2176]{1,0:T(8,128)S(1)}, u32[]{:S(2)}, u32[]{:S(2)}) %collective-permute-start.8) | collective-permute-done | bytes 69664 | tf_op jit(solution)/shard_map/ppermute | solution.py:178
  30.7 1.6 %collective-permute-start.11 = (f32[8,2176]{1,0:T(8,128)S(1)}, f32[8,2176]{1,0:T(8,128)S(1)}, u32[]{:S(2)}, u32[]{:S(2)}) collective-permute-start(f32[8,2176]{1,0:T(8,128)S(1)} %add.28), channel_id=1, source_target_pairs={{0,24},{4,28},{8,16},{12,20},{16,8},{20,12},{24,0},{28,4},{1,25},{... | collective-permute-start | bytes 208904 | tf_op jit(solution)/shard_map/ppermute | solution.py:178
  32.3 0.9 %collective-permute-start.10 = (f32[8,2176]{1,0:T(8,128)S(1)}, f32[8,2176]{1,0:T(8,128)S(1)}, u32[]{:S(2)}, u32[]{:S(2)}) collective-permute-start(f32[8,2176]{1,0:T(8,128)S(1)} %add.28), channel_id=1, source_target_pairs={{0,16},{4,20},{8,24},{12,28},{16,0},{20,4},{24,8},{28,12},{1,17},{... | collective-permute-start | bytes 208904 | tf_op jit(solution)/shard_map/ppermute | solution.py:178
  33.2 1.1 %collective-permute-start.9 = (f32[8,2176]{1,0:T(8,128)S(1)}, f32[8,2176]{1,0:T(8,128)S(1)}, u32[]{:S(2)}, u32[]{:S(2)}) collective-permute-start(f32[8,2176]{1,0:T(8,128)S(1)} %add.28), channel_id=1, source_target_pairs={{0,8},{4,12},{8,0},{12,4},{16,24},{20,28},{24,16},{28,20},{1,9},{5... | collective-permute-start | bytes 208904 | tf_op jit(solution)/shard_map/ppermute | solution.py:178
  34.3 1.8 %collective-permute-done.11 = f32[8,2176]{1,0:T(8,128)S(1)} collective-permute-done((f32[8,2176]{1,0:T(8,128)S(1)}, f32[8,2176]{1,0:T(8,128)S(1)}, u32[]{:S(2)}, u32[]{:S(2)}) %collective-permute-start.11) | collective-permute-done | bytes 69664 | tf_op jit(solution)/shard_map/ppermute | solution.py:178
  36.1 1.3 %collective-permute-done.10 = f32[8,2176]{1,0:T(8,128)S(1)} collective-permute-done((f32[8,2176]{1,0:T(8,128)S(1)}, f32[8,2176]{1,0:T(8,128)S(1)}, u32[]{:S(2)}, u32[]{:S(2)}) %collective-permute-start.10) | collective-permute-done | bytes 69664 | tf_op jit(solution)/shard_map/ppermute | solution.py:178
  37.4 0.1 collective-permute-done.9
  37.6 0.1 collective-permute-start.12
  37.7 1.2 %collective-permute-done.12.mate = f32[8,2176]{1,0:T(8,128)S(1)} collective-permute-done((f32[8,2176]{1,0:T(8,128)S(1)}, f32[8,2176]{1,0:T(8,128)S(1)}, u32[]{:S(2)}, u32[]{:S(2)}) %collective-permute-start.12) | collective-permute-done | bytes 69664 | tf_op jit(solution)/shard_map/ppermute | solution.py:178
  38.9 0.2 columns.1
  39.1 1.7 %collective-permute-start.15 = (f32[8,128]{1,0:T(8,128)S(1)}, f32[8,128]{1,0:T(8,128)S(1)}, u32[]{:S(2)}, u32[]{:S(2)}) collective-permute-start(f32[8,128]{1,0:T(8,128)S(1)} %get-tuple-element.27.rest_0_), channel_id=1, source_target_pairs={{0,3},{1,2},{2,1},{3,0},{4,7},{5,6},{6,5},{7,4},{8,11},{9,10},{10,... | collective-permute-start | bytes 12296 | tf_op jit(solution)/shard_map/ppermute | solution.py:178
  40.8 0.4 collective-permute-start.14
  41.2 2.3 %collective-permute-start.13 = (f32[8,128]{1,0:T(8,128)S(1)}, f32[8,128]{1,0:T(8,128)S(1)}, u32[]{:S(2)}, u32[]{:S(2)}) collective-permute-start(f32[8,128]{1,0:T(8,128)S(1)} %get-tuple-element.27.rest_0_), channel_id=1, source_target_pairs={{0,1},{1,0},{2,3},{3,2},{4,5},{5,4},{6,7},{7,6},{8,9},{9,8},{10,11... | collective-permute-start | bytes 12296 | tf_op jit(solution)/shard_map/ppermute | solution.py:178
  43.5 1.0 %collective-permute-done.15.rest_3_ = f32[8,128]{1,0:T(8,128)S(1)} collective-permute-done((f32[8,128]{1,0:T(8,128)S(1)}, f32[8,128]{1,0:T(8,128)S(1)}, u32[]{:S(2)}, u32[]{:S(2)}) %collective-permute-start.15) | collective-permute-done | bytes 4128 | tf_op jit(solution)/shard_map/ppermute | solution.py:178
  44.5 0.8 %collective-permute-done.14.rest_2_ = f32[8,128]{1,0:T(8,128)S(1)} collective-permute-done((f32[8,128]{1,0:T(8,128)S(1)}, f32[8,128]{1,0:T(8,128)S(1)}, u32[]{:S(2)}, u32[]{:S(2)}) %collective-permute-start.14) | collective-permute-done | bytes 4128 | tf_op jit(solution)/shard_map/ppermute | solution.py:178
  45.3 0.0 collective-permute-done.13.rest_1_
  45.3 1.0 %combine.1 = (f32[8,1024]{1,0:T(8,128)}, f32[1,4096]{1,0:T(1,128)}) custom-call(f32[1]{0:T(128)S(6)} %copy.8.delta, f32[8,1024]{1,0:T(8,128)S(1)} %get-tuple-element.16.rhs, f32[8,1024]{1,0:T(8,128)S(1)} %get-tuple-element.21.residual, f32[8,128]{1,0:T(8,128)S(1)} %get-tuple-element.22.alpha, f32[8,2176]{1,0:T(8,128)S(1)} %add_add_fusion.1.own.first, ...), custom_call_target="tpu_custom_call" | custom-call | tf_op jit(solution)/shard_map/combine/pallas_call | solution.py:245
  (4 shorter events, 0.1 us)
Async XLA Ops:
  0.6 16.7 %copy-start.1 = (f32[4096]{0:T(1024)S(1)}, f32[4096]{0:T(1024)}, u32[]{:S(2)}) copy-start(f32[4096]{0:T(1024)} %param.8) | copy-start | bytes 49156
  0.6 16.7 %copy-start = (f32[4096]{0:T(1024)S(1)}, f32[4096]{0:T(1024)}, u32[]{:S(2)}) copy-start(f32[4096]{0:T(1024)} %param.7) | copy-start | bytes 49156
  0.7 0.8 %copy-start.2 = (f32[1024,7]{0,1:T(8,128)S(1)}, f32[1024,7]{0,1:T(8,128)}, u32[]{:S(2)}) copy-start(f32[1024,7]{0,1:T(8,128)} %param.10) | copy-start | bytes 86020
  1.4 0.7 %copy-start.3 = (f32[1024]{0:T(1024)S(1)}, f32[1024]{0:T(1024)}, u32[]{:S(2)}) copy-start(f32[1024]{0:T(1024)} %param.9) | copy-start | bytes 12292
  5.8 1.4 %collective-permute-start = (f32[8,2176]{1,0:T(8,128)S(1)}, f32[8,2176]{1,0:T(8,128)S(1)}, u32[]{:S(2)}, u32[]{:S(2)}) collective-permute-start(f32[8,2176]{1,0:T(8,128)S(1)} %get-tuple-element.18), channel_id=1, source_target_pairs={{0,4},{4,0},{8,12},{12,8},{16,20},{20,16},{24,28},{28,24},{1,5},{5... | collective-permute-start | bytes 208904 | tf_op jit(solution)/shard_map/ppermute | solution.py:178
  7.3 6.4 %collective-permute-start.3 = (f32[8,2176]{1,0:T(8,128)S(1)}, f32[8,2176]{1,0:T(8,128)S(1)}, u32[]{:S(2)}, u32[]{:S(2)}) collective-permute-start(f32[8,2176]{1,0:T(8,128)S(1)} %add.24), channel_id=1, source_target_pairs={{0,24},{4,28},{8,16},{12,20},{16,8},{20,12},{24,0},{28,4},{1,25},{... | collective-permute-start | bytes 208904 | tf_op jit(solution)/shard_map/ppermute | solution.py:178
  11.1 4.3 %collective-permute-start.2 = (f32[8,2176]{1,0:T(8,128)S(1)}, f32[8,2176]{1,0:T(8,128)S(1)}, u32[]{:S(2)}, u32[]{:S(2)}) collective-permute-start(f32[8,2176]{1,0:T(8,128)S(1)} %add.24), channel_id=1, source_target_pairs={{0,16},{4,20},{8,24},{12,28},{16,0},{20,4},{24,8},{28,12},{1,17},{... | collective-permute-start | bytes 208904 | tf_op jit(solution)/shard_map/ppermute | solution.py:178
  11.7 4.3 %collective-permute-start.1 = (f32[8,2176]{1,0:T(8,128)S(1)}, f32[8,2176]{1,0:T(8,128)S(1)}, u32[]{:S(2)}, u32[]{:S(2)}) collective-permute-start(f32[8,2176]{1,0:T(8,128)S(1)} %add.24), channel_id=1, source_target_pairs={{0,8},{4,12},{8,0},{12,4},{16,24},{20,28},{24,16},{28,20},{1,9},{5... | collective-permute-start | bytes 208904 | tf_op jit(solution)/shard_map/ppermute | solution.py:178
  16.0 1.3 %collective-permute-start.4 = (f32[8,2176]{1,0:T(8,128)S(1)}, f32[8,2176]{1,0:T(8,128)S(1)}, u32[]{:S(2)}, u32[]{:S(2)}) collective-permute-start(f32[8,2176]{1,0:T(8,128)S(1)} %add_add_fusion.1.own.first), channel_id=1, source_target_pairs={{0,4},{4,0},{8,12},{12,8},{16,20},{20,16},{24,28},{28,24},{1,5},{5... | collective-permute-start | bytes 208904 | tf_op jit(solution)/shard_map/ppermute | solution.py:178
  19.6 5.8 %collective-permute-start.7 = (f32[8,1152]{1,0:T(8,128)S(1)}, f32[8,1152]{1,0:T(8,128)S(1)}, u32[]{:S(2)}, u32[]{:S(2)}) collective-permute-start(f32[8,1152]{1,0:T(8,128)S(1)} %get-tuple-element.20.rest_0_), channel_id=1, source_target_pairs={{0,3},{1,2},{2,1},{3,0},{4,7},{5,6},{6,5},{7,4},{8,11},{9,10},{10,... | collective-permute-start | bytes 110600 | tf_op jit(solution)/shard_map/ppermute | solution.py:178
  23.2 4.9 %collective-permute-start.6 = (f32[8,1152]{1,0:T(8,128)S(1)}, f32[8,1152]{1,0:T(8,128)S(1)}, u32[]{:S(2)}, u32[]{:S(2)}) collective-permute-start(f32[8,1152]{1,0:T(8,128)S(1)} %get-tuple-element.20.rest_0_), channel_id=1, source_target_pairs={{0,2},{1,3},{2,0},{3,1},{4,6},{5,7},{6,4},{7,5},{8,10},{9,11},{10,... | collective-permute-start | bytes 110600 | tf_op jit(solution)/shard_map/ppermute | solution.py:178
  23.2 4.9 %collective-permute-start.5 = (f32[8,1152]{1,0:T(8,128)S(1)}, f32[8,1152]{1,0:T(8,128)S(1)}, u32[]{:S(2)}, u32[]{:S(2)}) collective-permute-start(f32[8,1152]{1,0:T(8,128)S(1)} %get-tuple-element.20.rest_0_), channel_id=1, source_target_pairs={{0,1},{1,0},{2,3},{3,2},{4,5},{5,4},{6,7},{7,6},{8,9},{9,8},{10,11... | collective-permute-start | bytes 110600 | tf_op jit(solution)/shard_map/ppermute | solution.py:178
  29.5 1.3 %collective-permute-start.8 = (f32[8,2176]{1,0:T(8,128)S(1)}, f32[8,2176]{1,0:T(8,128)S(1)}, u32[]{:S(2)}, u32[]{:S(2)}) collective-permute-start(f32[8,2176]{1,0:T(8,128)S(1)} %get-tuple-element.24), channel_id=1, source_target_pairs={{0,4},{4,0},{8,12},{12,8},{16,20},{20,16},{24,28},{28,24},{1,5},{5... | collective-permute-start | bytes 208904 | tf_op jit(solution)/shard_map/ppermute | solution.py:178
  30.7 5.4 %collective-permute-start.11 = (f32[8,2176]{1,0:T(8,128)S(1)}, f32[8,2176]{1,0:T(8,128)S(1)}, u32[]{:S(2)}, u32[]{:S(2)}) collective-permute-start(f32[8,2176]{1,0:T(8,128)S(1)} %add.28), channel_id=1, source_target_pairs={{0,24},{4,28},{8,16},{12,20},{16,8},{20,12},{24,0},{28,4},{1,25},{... | collective-permute-start | bytes 208904 | tf_op jit(solution)/shard_map/ppermute | solution.py:178
  32.3 5.1 %collective-permute-start.10 = (f32[8,2176]{1,0:T(8,128)S(1)}, f32[8,2176]{1,0:T(8,128)S(1)}, u32[]{:S(2)}, u32[]{:S(2)}) collective-permute-start(f32[8,2176]{1,0:T(8,128)S(1)} %add.28), channel_id=1, source_target_pairs={{0,16},{4,20},{8,24},{12,28},{16,0},{20,4},{24,8},{28,12},{1,17},{... | collective-permute-start | bytes 208904 | tf_op jit(solution)/shard_map/ppermute | solution.py:178
  33.2 4.4 %collective-permute-start.9 = (f32[8,2176]{1,0:T(8,128)S(1)}, f32[8,2176]{1,0:T(8,128)S(1)}, u32[]{:S(2)}, u32[]{:S(2)}) collective-permute-start(f32[8,2176]{1,0:T(8,128)S(1)} %add.28), channel_id=1, source_target_pairs={{0,8},{4,12},{8,0},{12,4},{16,24},{20,28},{24,16},{28,20},{1,9},{5... | collective-permute-start | bytes 208904 | tf_op jit(solution)/shard_map/ppermute | solution.py:178
  37.6 1.3 %collective-permute-start.12 = (f32[8,2176]{1,0:T(8,128)S(1)}, f32[8,2176]{1,0:T(8,128)S(1)}, u32[]{:S(2)}, u32[]{:S(2)}) collective-permute-start(f32[8,2176]{1,0:T(8,128)S(1)} %add_add_fusion.own.second), channel_id=1, source_target_pairs={{0,4},{4,0},{8,12},{12,8},{16,20},{20,16},{24,28},{28,24},{1,5},{5... | collective-permute-start | bytes 208904 | tf_op jit(solution)/shard_map/ppermute | solution.py:178
  39.1 5.4 %collective-permute-start.15 = (f32[8,128]{1,0:T(8,128)S(1)}, f32[8,128]{1,0:T(8,128)S(1)}, u32[]{:S(2)}, u32[]{:S(2)}) collective-permute-start(f32[8,128]{1,0:T(8,128)S(1)} %get-tuple-element.27.rest_0_), channel_id=1, source_target_pairs={{0,3},{1,2},{2,1},{3,0},{4,7},{5,6},{6,5},{7,4},{8,11},{9,10},{10,... | collective-permute-start | bytes 12296 | tf_op jit(solution)/shard_map/ppermute | solution.py:178
  40.8 4.5 %collective-permute-start.14 = (f32[8,128]{1,0:T(8,128)S(1)}, f32[8,128]{1,0:T(8,128)S(1)}, u32[]{:S(2)}, u32[]{:S(2)}) collective-permute-start(f32[8,128]{1,0:T(8,128)S(1)} %get-tuple-element.27.rest_0_), channel_id=1, source_target_pairs={{0,2},{1,3},{2,0},{3,1},{4,6},{5,7},{6,4},{7,5},{8,10},{9,11},{10,... | collective-permute-start | bytes 12296 | tf_op jit(solution)/shard_map/ppermute | solution.py:178
  41.2 4.1 %collective-permute-start.13 = (f32[8,128]{1,0:T(8,128)S(1)}, f32[8,128]{1,0:T(8,128)S(1)}, u32[]{:S(2)}, u32[]{:S(2)}) collective-permute-start(f32[8,128]{1,0:T(8,128)S(1)} %get-tuple-element.27.rest_0_), channel_id=1, source_target_pairs={{0,1},{1,0},{2,3},{3,2},{4,5},{5,4},{6,7},{7,6},{8,9},{9,8},{10,11... | collective-permute-start | bytes 12296 | tf_op jit(solution)/shard_map/ppermute | solution.py:178
